TPU v7x, 256 devices: a whole 4x4x8 slice. The times are simulated.
256 devices in a mesh: hid: 64 (over y, z_hi, x), col: 4 (over z_lo, core).
Axes of the slice: x: 4, y: 4, z: 8 (z_hi: 4, z_lo: 2; z = z_hi * 2 + z_lo), core: 2. Of those that a mesh axis runs over, the one named last changes fastest.
Arguments:
- stream_a: bfloat16 [512, 8192], P('hid', 'col'), may hold values from -20 to 20
- stream_b: bfloat16 [512, 8192], P('hid', 'col'), may hold values from -20 to 20
- up_a: bfloat16 [8192, 28672], P('col', 'hid'), may hold values from -8 to 8
- up_b: bfloat16 [8192, 4, 7168], P('col', None, 'hid'), may hold values from -8 to 8
- gumbel: bfloat16 [28672, 28672], P('hid', 'col'), may hold values from -3 to 10
Outputs:
- row_pot: float32 [28672], P('hid')
- col_pot: float32 [4, 7168], P('col', 'hid')
All inputs are finite; a program needn't handle non-finite values.
Results may differ from a plain program's by a relative error of at most 0.0068.
Values may be sent and summed in bfloat16 or wider, within the bound.
No kernel may reach another device: no remote copies, remote signals or barrier semaphores. Data moves between devices by JAX's collectives and lax.ppermute only.
A program may use at most 128 MiB of HBM per device.

v0:
```python
import jax
import jax.numpy as jnp
from jax import lax
from jax.sharding import PartitionSpec as P

ITERS = 3


EPS = 1e-06
SHARPNESS = 32.0


def local(stream_a, stream_b, up_a, up_b, gumbel):
    tokens_a, tokens_b = (
        lax.all_gather(stream_a, "hid", axis=0, tiled=True),
        lax.all_gather(stream_b, "hid", axis=0, tiled=True),
    )
    count = tokens_a.shape[0]
    blocks = lax.axis_size("col")
    part_a = jnp.dot(tokens_a, up_a, preferred_element_type=jnp.float32)
    flat_b = up_b.reshape(up_b.shape[0], -1)
    part_b = jnp.dot(tokens_b, flat_b, preferred_element_type=jnp.float32).reshape(
        count, blocks, -1
    )
    act_a = lax.psum(part_a, "col").astype(jnp.bfloat16)
    act_b = lax.psum_scatter(part_b, "col", scatter_dimension=1, tiled=True).astype(jnp.bfloat16)
    act_b = act_b.reshape(count, -1)
    float_a = act_a.astype(jnp.float32)
    inv_a = lax.rsqrt(jnp.mean(float_a * float_a, axis=0) + EPS)
    scale = SHARPNESS / count
    piece = lax.all_gather(act_b, "hid", axis=1, tiled=True)
    float_b = piece.astype(jnp.float32)
    inv_b = lax.rsqrt(jnp.mean(float_b * float_b, axis=0) + EPS)
    cross = lax.dot_general(
        act_a, piece, (((0,), (0,)), ((), ())), preferred_element_type=jnp.float32
    )
    scores = scale * cross * inv_a[:, None] * inv_b[None, :]
    logits = scores + gumbel.astype(jnp.float32)
    width = logits.shape[1]
    share = width // lax.axis_size("hid")
    col_pot = jnp.zeros((width,), jnp.float32)
    row_pot = jnp.zeros((logits.shape[0],), jnp.float32)
    own_share = jnp.zeros((share,), jnp.float32)
    for step in range(ITERS):
        row_pot = -jnp.log(lax.psum(jnp.sum(jnp.exp(logits + col_pot[None, :]), axis=1), "col"))
        partial_value = jnp.sum(jnp.exp(logits + row_pot[:, None]), axis=0)
        col_pot = -jnp.log(lax.psum(partial_value, "hid"))
        own_share = lax.dynamic_slice_in_dim(col_pot, lax.axis_index("hid") * share, share)
    return (row_pot, own_share.reshape(1, share))


def solution(mesh):
    placed = (
        P("hid", "col"),
        P("hid", "col"),
        P("col", "hid"),
        P("col", None, "hid"),
        P("hid", "col"),
    )
    return jax.shard_map(
        local, mesh=mesh, in_specs=placed, out_specs=(P("hid"), P("col", "hid")), check_vma=False
    )
```

profile of v0, /device:TPU:32, one launch (start us, length us, event | category | flops | bytes accessed | tf_op | source)
XLA Modules:
  0.0 1499.5 jit_solution(2265144414115721725)
XLA Ops:
  7.2 0.7 all-gather.7.cloned.1.call-update
  8.0 83.5 %all-gather.7.cloned.1.call-done = bf16[512,2048]{1,0:T(8,128)(2,1)} async-done(((bf16[8,2048]{1,0:T(8,128)(2,1)}), bf16[512,2048]{1,0:T(8,128)(2,1)}) %all-gather.7.cloned.1.call-update) | async-done | bytes 2097168 | tf_op jit(solution)/shard_map/all_gather | solution.py:16
  91.5 3.7 fusion.1
  95.2 0.7 all-gather.5.cloned.1.call-update
  95.9 19.2 %reduce-scatter.2.cloned.1.call-done = f32[512,1,112]{0,2,1:T(8,128)} async-done(((f32[512,4,112]{0,2,1:T(8,128)}), f32[512,1,112]{0,2,1:T(8,128)}) %reduce-scatter.2.cloned.1.call-update) | async-done | bytes 229392 | tf_op jit(solution)/shard_map/reduce_scatter | solution.py:26
  115.1 1.6 convert_element_type.16
  116.7 81.1 %all-gather.5.cloned.1.call-done = bf16[512,2048]{1,0:T(8,128)(2,1)} async-done(((bf16[8,2048]{1,0:T(8,128)(2,1)}), bf16[512,2048]{1,0:T(8,128)(2,1)}) %all-gather.5.cloned.1.call-update) | async-done | bytes 2097168 | tf_op jit(solution)/shard_map/all_gather | solution.py:15
  197.8 3.3 fusion.7
  201.1 22.2 %all-reduce.1 = bf16[512,448]{0,1:T(8,128)(2,1)S(1)} all-reduce(f32[512,448]{0,1:T(8,128)S(1)} %fusion.7), channel_id=1, replica_groups=mesh['hid'=64,'col'=4] {'col'}, use_global_device_ids=true, to_apply=%region_0.0 | all-reduce | flops 229376 | bytes 1376256 | tf_op jit(solution)/shard_map/psum | solution.py:25
  223.5 84.3 %all-gather.9.cloned.1.call-done = bf16[512,1,7168]{0,2,1:T(8,128)(2,1)} async-done(((bf16[512,1,112]{0,2,1:T(8,128)(2,1)}), bf16[512,1,7168]{0,2,1:T(8,128)(2,1)}) %all-gather.9.cloned.1.call-update) | async-done | bytes 7340048 | tf_op jit(solution)/shard_map/all_gather | solution.py:31
  307.8 4.6 multiply_reduce_fusion
  312.4 10.2 exponential_reduce_fusion.5
  322.6 5.7 psum.50
  328.3 6.9 exponential_reduce_fusion.4
  335.2 377.8 %psum.51 = f32[7168]{0:T(1024)S(1)} all-reduce(f32[7168]{0:T(1024)S(1)} %exponential_reduce_fusion.4), channel_id=1, replica_groups=mesh['hid'=64,'col'=4] {'hid'}, use_global_device_ids=true, to_apply=%region_7.0 | all-reduce | flops 7168 | bytes 57344 | tf_op jit(solution)/shard_map/psum | solution.py:47
  713.0 6.6 exponential_reduce_fusion.3
  719.6 5.9 psum.52
  725.5 6.9 exponential_reduce_fusion.2
  732.4 370.3 %psum.53 = f32[7168]{0:T(1024)S(1)} all-reduce(f32[7168]{0:T(1024)S(1)} %exponential_reduce_fusion.2), channel_id=1, replica_groups=mesh['hid'=64,'col'=4] {'hid'}, use_global_device_ids=true, to_apply=%region_11.0 | all-reduce | flops 7168 | bytes 57344 | tf_op jit(solution)/shard_map/psum | solution.py:47
  1102.7 6.6 exponential_reduce_fusion.1
  1109.2 5.8 psum.54
  1115.0 6.9 exponential_reduce_fusion
  1121.9 370.4 %psum.55 = f32[7168]{0:T(1024)S(1)} all-reduce(f32[7168]{0:T(1024)S(1)} %exponential_reduce_fusion), channel_id=1, replica_groups=mesh['hid'=64,'col'=4] {'hid'}, use_global_device_ids=true, to_apply=%region_15.0 | all-reduce | flops 7168 | bytes 57344 | tf_op jit(solution)/shard_map/psum | solution.py:47
  1492.3 0.6 fusion.6
  (18 shorter events, 0.4 us)
Async XLA Ops:
  7.2 84.3 %copy-start = (bf16[2048,4,112]{0,2,1:T(8,128)(2,1)S(1)}, bf16[2048,4,112]{0,2,1:T(8,128)(2,1)}, u32[]{:S(2)}) copy-start(bf16[2048,4,112]{0,2,1:T(8,128)(2,1)} %param.8) | copy-start | bytes 5505028
  7.2 84.3 %all-gather.7.cloned.1.call-start = ((), (), s32[]{:S(2)}) async-start(), calls=%async_computation.2 | async-start | bytes 2129920 | tf_op jit(solution)/shard_map/all_gather | solution.py:16
  7.9 107.2 %reduce-scatter.2.cloned.1.call-start = ((), (), s32[]{:S(2)}) async-start(), calls=%async_computation.3 | async-start | bytes 1146880 | tf_op jit(solution)/shard_map/reduce_scatter | solution.py:26
  95.2 102.7 %all-gather.5.cloned.1.call-start = ((), (), s32[]{:S(2)}) async-start(), calls=%async_computation.1 | async-start | bytes 2129920 | tf_op jit(solution)/shard_map/all_gather | solution.py:15
  95.9 211.9 %all-gather.9.cloned.1.call-start = ((), (), s32[]{:S(2)}) async-start(), calls=%async_computation.4 | async-start | bytes 7454720 | tf_op jit(solution)/shard_map/all_gather | solution.py:31
  1115.0 377.9 %copy-start.1 = (f32[448]{0:T(512)}, f32[448]{0:T(512)S(1)}, u32[]{:S(2)}) copy-start(f32[448]{0:T(512)S(1)} %log_negate_fusion.2) | copy-start | bytes 5380
Sparse Core Ops, SparseCore 0:
  11.3 80.0 all-gather.6
  95.3 19.7 reduce-scatter.1
  118.4 79.3 all-gather.4
  201.0 106.7 all-gather.8
where the time goes:
time: 1500 us
  blocking collectives  1160 us (77%)
  waiting for transfers between devices  269 us (18%)
  other arithmetic  40.7 us (3%)
  matrix products  17.1 us (1%)
    psum x3, blocking collectives, local(): col_pot = -jnp.log(lax.psum(partial_value, 'hid'))  1120 us
    all_gather x1, waiting for transfers between devices, local(): piece = lax.all_gather(act_b, 'hid', axis=1, tiled=True)  84.3 us
    all_gather x1, waiting for transfers between devices, local(): lax.all_gather(stream_b, 'hid', axis=0, tiled=True)  83.5 us
    all_gather x1, waiting for transfers between devices, local(): lax.all_gather(stream_a, 'hid', axis=0, tiled=True)  81.1 us
  transfers between devices with their start and end apart: 4, of which 4 were waited for; matrix products, arithmetic and copies ran while one was open for 0% of the time, Pallas kernels for 0%

commit v1 on v0

v1 whole, which is shorter than its diff:
```python
import jax
import jax.numpy as jnp
from jax import lax
from jax.sharding import Mesh, PartitionSpec as P

ITERS = 3


EPS = 1e-06
SHARPNESS = 32.0

HID = ("y", "zh", "x")
COL = ("zl", "core")


def axis_sum(value, axis):
    size = lax.axis_size(axis)
    arrived = [
        lax.ppermute(value, axis, [(i, (i + shift) % size) for i in range(size)])
        for shift in range(1, size)
    ]
    for piece in arrived:
        value = value + piece
    return value


def hid_sum(value):
    for axis in ("x", "zh", "y"):
        value = axis_sum(value, axis)
    return value


def hid_gather(value, axis):
    for name in ("x", "zh", "y"):
        value = lax.all_gather(value, name, axis=axis, tiled=True)
    return value


def local(stream_a, stream_b, up_a, up_b, gumbel):
    tokens_b = hid_gather(stream_b, 0)
    tokens_a = hid_gather(stream_a, 0)
    count = tokens_a.shape[0]
    blocks = lax.axis_size(COL)
    part_a = jnp.dot(tokens_a, up_a, preferred_element_type=jnp.float32)
    flat_b = up_b.reshape(up_b.shape[0], -1)
    part_b = jnp.dot(tokens_b, flat_b, preferred_element_type=jnp.float32).reshape(
        count, blocks, -1
    )
    act_a = lax.psum(part_a, COL).astype(jnp.bfloat16)
    act_b = lax.psum_scatter(part_b, COL, scatter_dimension=1, tiled=True).astype(jnp.bfloat16)
    act_b = act_b.reshape(count, -1)
    float_a = act_a.astype(jnp.float32)
    inv_a = lax.rsqrt(jnp.mean(float_a * float_a, axis=0) + EPS)
    scale = SHARPNESS / count
    piece = hid_gather(act_b.T, 0).T
    float_b = piece.astype(jnp.float32)
    inv_b = lax.rsqrt(jnp.mean(float_b * float_b, axis=0) + EPS)
    cross = lax.dot_general(
        act_a, piece, (((0,), (0,)), ((), ())), preferred_element_type=jnp.float32
    )
    scores = scale * cross * inv_a[:, None] * inv_b[None, :]
    logits = scores + gumbel.astype(jnp.float32)
    width = logits.shape[1]
    share = width // lax.axis_size(HID)
    col_pot = jnp.zeros((width,), jnp.float32)
    row_pot = jnp.zeros((logits.shape[0],), jnp.float32)
    for step in range(ITERS):
        row_pot = -jnp.log(axis_sum(jnp.sum(jnp.exp(logits + col_pot[None, :]), axis=1), COL))
        partial_value = jnp.sum(jnp.exp(logits + row_pot[:, None]), axis=0)
        col_pot = -jnp.log(hid_sum(partial_value))
    own_share = lax.dynamic_slice_in_dim(col_pot, lax.axis_index(HID) * share, share)
    return (row_pot, own_share.reshape(1, share))


def solution(mesh):
    fine = Mesh(mesh.devices.reshape(4, 4, 4, 2, 2), HID + COL)
    placed = (
        P(HID, COL),
        P(HID, COL),
        P(COL, HID),
        P(COL, None, HID),
        P(HID, COL),
    )
    return jax.shard_map(
        local, mesh=fine, in_specs=placed, out_specs=(P(HID), P(COL, HID)), check_vma=False
    )
```

time: 1500 us -> 416 us (0.28)
  blocking collectives: 1160 us -> 114 us
  waiting for transfers between devices: 269 us -> 181 us
  starting transfers between devices: 0.16 us -> 68.2 us
  other arithmetic: 40.7 us -> 18.1 us
    psum x7 -> x1, blocking collectives: 1160 us -> 20.7 us  [local(): act_a = lax.psum(part_a, COL).astype(jnp.bfloat16)]
    all_gather x3 -> x4, waiting for transfers between devices: 249 us -> 129 us  [hid_gather(): value = lax.all_gather(value, name, axis=axis, tiled=True)]
    all_gather x0 -> x5, blocking collectives: none -> 93.8 us  [hid_gather(): value = lax.all_gather(value, name, axis=axis, tiled=True)]
    ppermute x0 -> x36, starting transfers between devices: none -> 68 us  [axis_sum(): lax.ppermute(value, axis, [(i, (i + shift) % size) for i in range(size)])]
    ppermute x0 -> x36, waiting for transfers between devices: none -> 31.6 us  [axis_sum(): lax.ppermute(value, axis, [(i, (i + shift) % size) for i in range(size)])]
  transfers between devices with their start and end apart: 4 -> 41, of which waited for: 4 -> 35; matrix products, arithmetic and copies ran while one was open for 0% -> 1% of each run, Pallas kernels for 0% -> 0%
where the time goes in v1:
time: 416 us; the launch traced here: 411 us
  waiting for transfers between devices  181 us (44%)
  blocking collectives  114 us (27%)
  starting transfers between devices  68.2 us (16%)
  other arithmetic  18.1 us (4%)
  matrix products  14.6 us (4%)
  between operations  14.2 us (3%)
    all_gather x4, waiting for transfers between devices, hid_gather(): value = lax.all_gather(value, name, axis=axis, tiled=True)  129 us
    all_gather x5, blocking collectives, hid_gather(): value = lax.all_gather(value, name, axis=axis, tiled=True)  93.8 us
    ppermute x36, starting transfers between devices, axis_sum(): lax.ppermute(value, axis, [(i, (i + shift) % size) for i in range(size)])  68 us
    ppermute x36, waiting for transfers between devices, axis_sum(): lax.ppermute(value, axis, [(i, (i + shift) % size) for i in range(size)])  31.6 us
    reduce_scatter x1, waiting for transfers between devices, local(): lax.psum_scatter(part_b, COL, scatter_dimension=1, tiled=True)  20.8 us
    psum x1, blocking collectives, local(): act_a = lax.psum(part_a, COL).astype(jnp.bfloat16)  20.7 us
  transfers between devices with their start and end apart: 41, of which 35 were waited for; matrix products, arithmetic and copies ran while one was open for 1% of the time, Pallas kernels for 0%

profile of v1, /device:TPU:32, one launch (start us, length us, event | category | flops | bytes accessed | tf_op | source)
XLA Modules:
  0.0 410.9 jit_solution(1137617978926640542)
XLA Ops:
  7.2 12.7 %all_gather.30 = bf16[32,2048]{1,0:T(8,128)(2,1)S(1)} all-gather(bf16[8,2048]{1,0:T(8,128)(2,1)} %param.6), channel_id=1, replica_groups=mesh['y'=4,'zh'=4,'x'=4,'zl'=2,'core'=2] {'x'}, dimensions={0}, use_global_device_ids=true | all-gather | bytes 163840 | tf_op jit(solution)/shard_map/all_gather | solution.py:35
  19.9 20.2 %all_gather.31 = bf16[128,2048]{1,0:T(8,128)(2,1)} all-gather(bf16[32,2048]{1,0:T(8,128)(2,1)S(1)} %all_gather.30), channel_id=1, replica_groups=mesh['y'=4,'zh'=4,'x'=4,'zl'=2,'core'=2] {'zh'}, dimensions={0}, use_global_device_ids=true | all-gather | bytes 655360 | tf_op jit(solution)/shard_map/all_gather | solution.py:35
  40.2 31.7 %all-gather.7.cloned.1.call-done = bf16[512,2048]{1,0:T(8,128)(2,1)} async-done(((bf16[128,2048]{1,0:T(8,128)(2,1)}), bf16[512,2048]{1,0:T(8,128)(2,1)}) %all-gather.7.cloned.1.call-update) | async-done | bytes 2097168 | tf_op jit(solution)/shard_map/all_gather | solution.py:35
  71.9 3.7 fusion
  75.7 20.8 %reduce-scatter.2.cloned.1.call-done = f32[512,1,112]{0,2,1:T(8,128)} async-done(((f32[512,4,112]{0,2,1:T(8,128)}), f32[512,1,112]{0,2,1:T(8,128)}) %reduce-scatter.2.cloned.1.call-update) | async-done | bytes 229392 | tf_op jit(solution)/shard_map/reduce_scatter | solution.py:50
  97.5 14.2 %all_gather.33 = bf16[448,512]{1,0:T(8,128)(2,1)} all-gather(bf16[112,512]{1,0:T(8,128)(2,1)S(1)} %convert_bitcast_fusion), channel_id=1, replica_groups=mesh['y'=4,'zh'=4,'x'=4,'zl'=2,'core'=2] {'x'}, dimensions={0}, use_global_device_ids=true | all-gather | bytes 573440 | tf_op jit(solution)/shard_map/all_gather | solution.py:35
  111.8 12.3 %all_gather.27 = bf16[32,2048]{1,0:T(8,128)(2,1)S(1)} all-gather(bf16[8,2048]{1,0:T(8,128)(2,1)} %param.5), channel_id=1, replica_groups=mesh['y'=4,'zh'=4,'x'=4,'zl'=2,'core'=2] {'x'}, dimensions={0}, use_global_device_ids=true | all-gather | bytes 163840 | tf_op jit(solution)/shard_map/all_gather | solution.py:35
  124.1 34.4 %all_gather.28 = bf16[128,2048]{1,0:T(8,128)(2,1)} all-gather(bf16[32,2048]{1,0:T(8,128)(2,1)S(1)} %all_gather.27), channel_id=1, replica_groups=mesh['y'=4,'zh'=4,'x'=4,'zl'=2,'core'=2] {'zh'}, dimensions={0}, use_global_device_ids=true | all-gather | bytes 655360 | tf_op jit(solution)/shard_map/all_gather | solution.py:35
  158.5 7.9 %all-gather.9.cloned.1.call-done = bf16[1792,512]{1,0:T(8,128)(2,1)} async-done(((bf16[448,512]{1,0:T(8,128)(2,1)}), bf16[1792,512]{1,0:T(8,128)(2,1)}) %all-gather.9.cloned.1.call-update) | async-done | bytes 1835024 | tf_op jit(solution)/shard_map/all_gather | solution.py:35
  166.4 34.8 %all-gather.5.cloned.1.call-done = bf16[512,2048]{1,0:T(8,128)(2,1)} async-done(((bf16[128,2048]{1,0:T(8,128)(2,1)}), bf16[512,2048]{1,0:T(8,128)(2,1)}) %all-gather.5.cloned.1.call-update) | async-done | bytes 2097168 | tf_op jit(solution)/shard_map/all_gather | solution.py:35
  201.1 3.3 fusion.5
  204.4 20.7 %all-reduce.1 = bf16[512,448]{0,1:T(8,128)(2,1)S(1)} all-reduce(f32[512,448]{0,1:T(8,128)S(1)} %fusion.5), channel_id=1, replica_groups=mesh['y'=4,'zh'=4,'x'=4,'zl'=2,'core'=2] {'zl','core'}, use_global_device_ids=true, to_apply=%region_0.0 | all-reduce | flops 229376 | bytes 1376256 | tf_op jit(solution)/shard_map/psum | solution.py:49
  225.3 54.5 %all-gather.11.cloned.1.call-done = bf16[7168,512]{1,0:T(8,128)(2,1)} async-done(((bf16[1792,512]{1,0:T(8,128)(2,1)}), bf16[7168,512]{1,0:T(8,128)(2,1)}) %all-gather.11.cloned.1.call-update) | async-done | bytes 7340048 | tf_op jit(solution)/shard_map/all_gather | solution.py:35
  279.9 4.6 %multiply_reduce_fusion = f32[7168]{0:T(1024)S(1)} fusion(bf16[7168,512]{1,0:T(8,128)(2,1)} %all-gather.11.cloned.1.call-done), kind=kLoop, calls=%fused_computation | loop fusion | flops 11002880 | bytes 7368704 | tf_op jit(solution)/shard_map/reduce_sum | solution.py:57
  284.5 7.6 %exponential_reduce_fusion.5 = (f32[448]{0:T(512)S(1)}, f32[448,7168]{1,0:T(8,128)S(1)}) fusion(bf16[448,7168]{1,0:T(8,128)(2,1)} %param.9, f32[7168]{0:T(1024)S(1)} %add_rsqrt_fusion, f32[448]{0:T(512)S(1)} %rsqrt_multiply_fusion, bf16[512,448]{0,1:T(8,128)(2,1)S(1)} %all-reduce.1, bf16[7168,512]{1,0:T(8,128)(2,1)} %all-gather.11.cloned.1.call-done), kind=kOutput, calls=%fused_computation.6 | convolution fusion | flops 3304390144 | bytes 27098624 | tf_op jit(solution)/shard_map/dot_general | solution.py:58
  309.5 3.5 collective-permute-start.7
  313.0 3.4 collective-permute-start.8
  335.9 9.6 %collective-permute-start.15 = (f32[7168]{0:T(1024)S(1)}, f32[7168]{0:T(1024)S(1)}, u32[]{:S(2)}, u32[]{:S(2)}) collective-permute-start(f32[7168]{0:T(1024)S(1)} %exponential_reduce_fusion.2), channel_id=1, source_target_pairs={{0,4},{4,8},{8,12},{12,0},{1,5},{5,9},{9,13},{13,1},{2,6},{6,10},{... | collective-permute-start | bytes 86024 | tf_op jit(solution)/shard_map/ppermute | solution.py:19
  345.4 3.5 collective-permute-start.16
  355.2 4.0 collective-permute-start.19
  359.9 3.5 collective-permute-done.19
  379.2 2.7 collective-permute-start.28
  387.4 3.1 collective-permute-start.31
  390.5 2.9 collective-permute-start.32
  (98 shorter events, 77.0 us)
Async XLA Ops:
  7.2 64.8 %all-gather.7.cloned.1.call-start = ((), (), s32[]{:S(2)}) async-start(), calls=%async_computation.2 | async-start | bytes 2621440 | tf_op jit(solution)/shard_map/all_gather | solution.py:35
  40.2 56.4 %reduce-scatter.2.cloned.1.call-start = ((), (), s32[]{:S(2)}) async-start(), calls=%async_computation.3 | async-start | bytes 1146880 | tf_op jit(solution)/shard_map/reduce_scatter | solution.py:50
  75.6 90.7 %all-gather.9.cloned.1.call-start = ((), (), s32[]{:S(2)}) async-start(), calls=%async_computation.4 | async-start | bytes 2293760 | tf_op jit(solution)/shard_map/all_gather | solution.py:35
  111.7 89.4 %all-gather.5.cloned.1.call-start = ((), (), s32[]{:S(2)}) async-start(), calls=%async_computation.1 | async-start | bytes 2621440 | tf_op jit(solution)/shard_map/all_gather | solution.py:35
  158.5 121.4 %all-gather.11.cloned.1.call-start = ((), (), s32[]{:S(2)}) async-start(), calls=%async_computation.5 | async-start | bytes 9175040 | tf_op jit(solution)/shard_map/all_gather | solution.py:35
  298.5 5.9 %collective-permute-start.3 = (f32[7168]{0:T(1024)S(1)}, f32[7168]{0:T(1024)S(1)}, u32[]{:S(2)}, u32[]{:S(2)}) collective-permute-start(f32[7168]{0:T(1024)S(1)} %exponential_reduce_fusion.4), channel_id=1, source_target_pairs={{0,4},{4,8},{8,12},{12,0},{1,5},{5,9},{9,13},{13,1},{2,6},{6,10},{... | collective-permute-start | bytes 86024 | tf_op jit(solution)/shard_map/ppermute | solution.py:19
  300.3 5.6 %collective-permute-start.4 = (f32[7168]{0:T(1024)S(1)}, f32[7168]{0:T(1024)S(1)}, u32[]{:S(2)}, u32[]{:S(2)}) collective-permute-start(f32[7168]{0:T(1024)S(1)} %exponential_reduce_fusion.4), channel_id=1, source_target_pairs={{0,8},{4,12},{8,0},{12,4},{1,9},{5,13},{9,1},{13,5},{2,10},{6,14},... | collective-permute-start | bytes 86024 | tf_op jit(solution)/shard_map/ppermute | solution.py:19
  306.9 9.5 %collective-permute-start.6 = (f32[7168]{0:T(1024)S(1)}, f32[7168]{0:T(1024)S(1)}, u32[]{:S(2)}, u32[]{:S(2)}) collective-permute-start(f32[7168]{0:T(1024)S(1)} %add_add_fusion.5), channel_id=1, source_target_pairs={{0,16},{16,32},{32,48},{48,0},{1,17},{17,33},{33,49},{49,1},{2,18}... | collective-permute-start | bytes 86024 | tf_op jit(solution)/shard_map/ppermute | solution.py:19
  309.5 7.9 %collective-permute-start.7 = (f32[7168]{0:T(1024)S(1)}, f32[7168]{0:T(1024)S(1)}, u32[]{:S(2)}, u32[]{:S(2)}) collective-permute-start(f32[7168]{0:T(1024)S(1)} %add_add_fusion.5), channel_id=1, source_target_pairs={{0,32},{16,48},{32,0},{48,16},{1,33},{17,49},{33,1},{49,17},{2,34}... | collective-permute-start | bytes 86024 | tf_op jit(solution)/shard_map/ppermute | solution.py:19
  318.0 5.5 %collective-permute-start.10 = (f32[7168]{0:T(1024)S(1)}, f32[7168]{0:T(1024)S(1)}, u32[]{:S(2)}, u32[]{:S(2)}) collective-permute-start(f32[7168]{0:T(1024)S(1)} %add_add_fusion.4), channel_id=1, source_target_pairs={{0,128},{64,192},{128,0},{192,64},{1,129},{65,193},{129,1},{193,65... | collective-permute-start | bytes 86024 | tf_op jit(solution)/shard_map/ppermute | solution.py:19
  322.0 5.1 %collective-permute-start.9 = (f32[7168]{0:T(1024)S(1)}, f32[7168]{0:T(1024)S(1)}, u32[]{:S(2)}, u32[]{:S(2)}) collective-permute-start(f32[7168]{0:T(1024)S(1)} %add_add_fusion.4), channel_id=1, source_target_pairs={{0,64},{64,128},{128,192},{192,0},{1,65},{65,129},{129,193},{193,1... | collective-permute-start | bytes 86024 | tf_op jit(solution)/shard_map/ppermute | solution.py:19
  335.9 14.1 %collective-permute-start.15 = (f32[7168]{0:T(1024)S(1)}, f32[7168]{0:T(1024)S(1)}, u32[]{:S(2)}, u32[]{:S(2)}) collective-permute-start(f32[7168]{0:T(1024)S(1)} %exponential_reduce_fusion.2), channel_id=1, source_target_pairs={{0,4},{4,8},{8,12},{12,0},{1,5},{5,9},{9,13},{13,1},{2,6},{6,10},{... | collective-permute-start | bytes 86024 | tf_op jit(solution)/shard_map/ppermute | solution.py:19
  345.4 6.1 %collective-permute-start.16 = (f32[7168]{0:T(1024)S(1)}, f32[7168]{0:T(1024)S(1)}, u32[]{:S(2)}, u32[]{:S(2)}) collective-permute-start(f32[7168]{0:T(1024)S(1)} %exponential_reduce_fusion.2), channel_id=1, source_target_pairs={{0,8},{4,12},{8,0},{12,4},{1,9},{5,13},{9,1},{13,5},{2,10},{6,14},... | collective-permute-start | bytes 86024 | tf_op jit(solution)/shard_map/ppermute | solution.py:19
  352.8 7.0 %collective-permute-start.18 = (f32[7168]{0:T(1024)S(1)}, f32[7168]{0:T(1024)S(1)}, u32[]{:S(2)}, u32[]{:S(2)}) collective-permute-start(f32[7168]{0:T(1024)S(1)} %add_add_fusion.3), channel_id=1, source_target_pairs={{0,16},{16,32},{32,48},{48,0},{1,17},{17,33},{33,49},{49,1},{2,18}... | collective-permute-start | bytes 86024 | tf_op jit(solution)/shard_map/ppermute | solution.py:19
  355.2 8.2 %collective-permute-start.19 = (f32[7168]{0:T(1024)S(1)}, f32[7168]{0:T(1024)S(1)}, u32[]{:S(2)}, u32[]{:S(2)}) collective-permute-start(f32[7168]{0:T(1024)S(1)} %add_add_fusion.3), channel_id=1, source_target_pairs={{0,32},{16,48},{32,0},{48,16},{1,33},{17,49},{33,1},{49,17},{2,34}... | collective-permute-start | bytes 86024 | tf_op jit(solution)/shard_map/ppermute | solution.py:19
  364.0 5.2 %collective-permute-start.21 = (f32[7168]{0:T(1024)S(1)}, f32[7168]{0:T(1024)S(1)}, u32[]{:S(2)}, u32[]{:S(2)}) collective-permute-start(f32[7168]{0:T(1024)S(1)} %add_add_fusion.2), channel_id=1, source_target_pairs={{0,64},{64,128},{128,192},{192,0},{1,65},{65,129},{129,193},{193,1... | collective-permute-start | bytes 86024 | tf_op jit(solution)/shard_map/ppermute | solution.py:19
  364.1 5.5 %collective-permute-start.22 = (f32[7168]{0:T(1024)S(1)}, f32[7168]{0:T(1024)S(1)}, u32[]{:S(2)}, u32[]{:S(2)}) collective-permute-start(f32[7168]{0:T(1024)S(1)} %add_add_fusion.2), channel_id=1, source_target_pairs={{0,128},{64,192},{128,0},{192,64},{1,129},{65,193},{129,1},{193,65... | collective-permute-start | bytes 86024 | tf_op jit(solution)/shard_map/ppermute | solution.py:19
  378.9 6.3 %collective-permute-start.27 = (f32[7168]{0:T(1024)S(1)}, f32[7168]{0:T(1024)S(1)}, u32[]{:S(2)}, u32[]{:S(2)}) collective-permute-start(f32[7168]{0:T(1024)S(1)} %exponential_reduce_fusion), channel_id=1, source_target_pairs={{0,4},{4,8},{8,12},{12,0},{1,5},{5,9},{9,13},{13,1},{2,6},{6,10},{... | collective-permute-start | bytes 86024 | tf_op jit(solution)/shard_map/ppermute | solution.py:19
  379.2 6.0 %collective-permute-start.28 = (f32[7168]{0:T(1024)S(1)}, f32[7168]{0:T(1024)S(1)}, u32[]{:S(2)}, u32[]{:S(2)}) collective-permute-start(f32[7168]{0:T(1024)S(1)} %exponential_reduce_fusion), channel_id=1, source_target_pairs={{0,8},{4,12},{8,0},{12,4},{1,9},{5,13},{9,1},{13,5},{2,10},{6,14},... | collective-permute-start | bytes 86024 | tf_op jit(solution)/shard_map/ppermute | solution.py:19
  385.8 7.6 %collective-permute-start.30 = (f32[7168]{0:T(1024)S(1)}, f32[7168]{0:T(1024)S(1)}, u32[]{:S(2)}, u32[]{:S(2)}) collective-permute-start(f32[7168]{0:T(1024)S(1)} %add_add_fusion.1), channel_id=1, source_target_pairs={{0,16},{16,32},{32,48},{48,0},{1,17},{17,33},{33,49},{49,1},{2,18}... | collective-permute-start | bytes 86024 | tf_op jit(solution)/shard_map/ppermute | solution.py:19
  387.4 8.1 %collective-permute-start.31 = (f32[7168]{0:T(1024)S(1)}, f32[7168]{0:T(1024)S(1)}, u32[]{:S(2)}, u32[]{:S(2)}) collective-permute-start(f32[7168]{0:T(1024)S(1)} %add_add_fusion.1), channel_id=1, source_target_pairs={{0,32},{16,48},{32,0},{48,16},{1,33},{17,49},{33,1},{49,17},{2,34}... | collective-permute-start | bytes 86024 | tf_op jit(solution)/shard_map/ppermute | solution.py:19
  390.5 5.3 %collective-permute-start.32 = (f32[7168]{0:T(1024)S(1)}, f32[7168]{0:T(1024)S(1)}, u32[]{:S(2)}, u32[]{:S(2)}) collective-permute-start(f32[7168]{0:T(1024)S(1)} %add_add_fusion.1), channel_id=1, source_target_pairs={{0,48},{16,0},{32,16},{48,32},{1,49},{17,1},{33,17},{49,33},{2,50}... | collective-permute-start | bytes 86024 | tf_op jit(solution)/shard_map/ppermute | solution.py:19
  395.8 5.2 %collective-permute-start.33 = (f32[7168]{0:T(1024)S(1)}, f32[7168]{0:T(1024)S(1)}, u32[]{:S(2)}, u32[]{:S(2)}) collective-permute-start(f32[7168]{0:T(1024)S(1)} %add_add_fusion), channel_id=1, source_target_pairs={{0,64},{64,128},{128,192},{192,0},{1,65},{65,129},{129,193},{193,1... | collective-permute-start | bytes 86024 | tf_op jit(solution)/shard_map/ppermute | solution.py:19
  397.6 5.4 %collective-permute-start.34 = (f32[7168]{0:T(1024)S(1)}, f32[7168]{0:T(1024)S(1)}, u32[]{:S(2)}, u32[]{:S(2)}) collective-permute-start(f32[7168]{0:T(1024)S(1)} %add_add_fusion), channel_id=1, source_target_pairs={{0,128},{64,192},{128,0},{192,64},{1,129},{65,193},{129,1},{193,65... | collective-permute-start | bytes 86024 | tf_op jit(solution)/shard_map/ppermute | solution.py:19
  (19 other events, 155.2 us)
Sparse Core Ops, SparseCore 0:
  40.3 31.6 all-gather.6
  75.8 20.7 reduce-scatter.1
  111.8 54.4 all-gather.8
  168.0 33.0 all-gather.4
  202.8 77.0 all-gather.10
